TPU v7x, 512 devices: a whole 4x8x8 slice. The times are simulated.
512 devices in a mesh: grp: 16 (over y_lo, x), chan: 32 (over y_hi, z, core).
Axes of the slice: x: 4, y: 8 (y_hi: 2, y_lo: 4; y = y_hi * 4 + y_lo), z: 8, core: 2. Of those that a mesh axis runs over, the one named last changes fastest.
Arguments:
- voltages: bfloat16 [512, 2, 2, 77824], P(('grp', 'chan')), may hold values from -6 to 6
- beam_weights: bfloat16 [512, 4096, 2, 128], P('grp', 'chan'), may hold values from -0.25 to 0.25
- owner_table: int32 [4096], replicated, may hold values from 0 to 4095, each once
- live_stations: int32 [512], P(('grp', 'chan')), may hold values 0 or 1
Outputs:
- beams: float32 [128, 2, 2, 4, 4096], P('grp', None, None, None, 'chan')
Inputs may be any that keep to these rules, and one draw needn't show every extreme that they name: `owner_table`: each of the 4096 channels appears exactly once.
All inputs are finite; a program needn't handle non-finite values. No bound on the sum of `live_stations` on one device may be relied on, other than what follows from the above.
Results may differ from a plain program's by a relative error of at most 0.02.
Values may be sent and summed in bfloat16 or wider, within the bound.
No kernel may reach another device: no remote copies, remote signals or barrier semaphores. Data moves between devices by JAX's collectives and lax.ppermute only.
A program may use at most 64 MiB of HBM per device.

v0:
```python
import math

import jax
import jax.numpy as jnp
from jax import lax
from jax.sharding import PartitionSpec as P

CHANNELS = 4096
TAPS = 16
BEAMS = 128
POLS = 2
FIRST = 4
SPECTRA = 4
SECOND = 1024


def prototype():
    total = TAPS * CHANNELS
    place = jnp.arange(total, dtype=jnp.int32).astype(jnp.float32)
    window = 0.54 - 0.46 * jnp.cos(2.0 * math.pi * place / total)
    centred = (place - float(total // 2)) / CHANNELS
    return (window * jnp.sinc(centred) / math.sqrt(CHANNELS)).reshape(TAPS, CHANNELS)


def section_table(length, modulus, dtype):
    points = jnp.arange(length, dtype=jnp.int32)
    angle = (
        2.0 * math.pi * (points[:, None] * points[None, :] % modulus).astype(jnp.float32) / modulus
    )
    cosine = jnp.cos(angle).astype(dtype)
    sine = jnp.sin(angle).astype(dtype)
    return jnp.stack([jnp.stack([cosine, -sine], 1), jnp.stack([sine, cosine], 1)], 0)


def channelize(volts):
    stations = volts.shape[0]
    frames = volts.reshape(stations, POLS, 2, SPECTRA + TAPS - 1, CHANNELS)
    coeffs = prototype()
    summed = jnp.zeros((stations, POLS, 2, SPECTRA, CHANNELS), jnp.float32)
    for tap_index in range(TAPS):
        summed = (
            summed
            + frames[:, :, :, tap_index : tap_index + SPECTRA, :].astype(jnp.float32)
            * coeffs[tap_index]
        )
    filtered = summed.astype(jnp.bfloat16)
    split = filtered.astype(jnp.float32).reshape(stations, POLS, 2, SPECTRA, FIRST, SECOND)
    first_table = section_table(FIRST, FIRST, jnp.float32)
    folded = jnp.einsum("gprsnm,rnqk->gpqskm", split, first_table, precision=lax.Precision.HIGHEST)
    low = jnp.arange(FIRST, dtype=jnp.int32)
    high = jnp.arange(SECOND, dtype=jnp.int32)
    angle = 2.0 * math.pi * (low[:, None] * high[None, :] % CHANNELS).astype(jnp.float32) / CHANNELS
    cosine = jnp.cos(angle)
    sine = jnp.sin(angle)
    real_in = folded[:, :, 0]
    imag_in = folded[:, :, 1]
    twisted = jnp.stack(
        [real_in * cosine + imag_in * sine, imag_in * cosine - real_in * sine], 2
    ).astype(jnp.bfloat16)
    second_table = section_table(SECOND, SECOND, jnp.bfloat16)
    spectra = jnp.einsum(
        "gprskn,rnqm->gpsqkm", twisted, second_table, preferred_element_type=jnp.float32
    )
    return spectra.reshape(stations, POLS, SPECTRA, 2, CHANNELS).astype(jnp.bfloat16)


def complex_weights(weights, axis):
    w_real = jnp.take(weights, 0, axis=axis)
    w_imag = jnp.take(weights, 1, axis=axis)
    upper_rows = jnp.stack([w_real, w_imag], axis)
    lower_rows = jnp.stack([-w_imag, w_real], axis)
    return jnp.stack([upper_rows, lower_rows], 0)


def shards(voltages, beam_weights, owner_table, live_stations):
    slot_index = owner_table % FIRST * SECOND + owner_table // FIRST
    spectra = channelize(voltages)
    spectra = (
        jnp.take(spectra, slot_index, axis=4)
        * live_stations.astype(jnp.bfloat16)[:, None, None, None, None]
    )
    turned = lax.all_to_all(spectra, "chan", split_axis=4, concat_axis=0, tiled=True)
    group_size = lax.axis_size("chan")
    group_count = lax.axis_size("grp")
    slot_width = turned.shape[4]
    rows_total = POLS * SPECTRA
    inputs = jnp.transpose(turned, (4, 1, 2, 3, 0)).reshape(slot_width, rows_total, 2 * group_size)
    stacked = complex_weights(beam_weights, 2)
    stacked = jnp.transpose(stacked, (2, 0, 1, 3, 4)).reshape(slot_width, 2 * group_size, 2, BEAMS)
    chosen = stacked
    chosen = chosen.reshape(
        slot_width, 2 * group_size, 2 * (BEAMS // group_count * lax.axis_size("grp"))
    )
    product = lax.dot_general(
        inputs, chosen, (((2,), (1,)), ((0,), (0,))), preferred_element_type=jnp.float32
    )
    product = product.reshape(
        slot_width, POLS, SPECTRA, 2, BEAMS // group_count * lax.axis_size("grp")
    )
    return lax.psum_scatter(
        jnp.transpose(product, (4, 3, 1, 2, 0)).astype(jnp.bfloat16),
        "grp",
        scatter_dimension=0,
        tiled=True,
    ).astype(jnp.float32)


def solution(mesh):
    in_specs = (
        P(("grp", "chan"), None, None, None),
        P("grp", "chan", None, None),
        P(),
        P(("grp", "chan")),
    )
    out_specs = P("grp", None, None, None, "chan")
    return jax.shard_map(shards, mesh=mesh, in_specs=in_specs, out_specs=out_specs, check_vma=False)
```

profile of v0, /device:TPU:2, one launch (start us, length us, event | category | flops | bytes accessed | tf_op | source)
XLA Modules:
  0.0 350.5 jit_solution(14879874654682418821)
XLA Ops:
  6.5 15.8 %fusion.11 = bf16[1024,1,1024]{2,0,1:T(8,128)(2,1)S(1)} fusion(), kind=kLoop, calls=%fused_computation.26 | loop fusion | flops 18874368 | bytes 2097152 | tf_op jit(solution)/shard_map/neg | solution.py:32
  22.4 17.7 %sine_convert_fusion = (bf16[1024,1,1024]{2,0,1:T(8,128)(2,1)}, bf16[1024,1,1024]{2,0,1:T(8,128)(2,1)}) fusion(), kind=kLoop, calls=%fused_computation.12 | loop fusion | flops 16777216 | bytes 4194304 | tf_op jit(solution)/shard_map/convert_element_type | solution.py:31
  40.1 0.1 fusion.44
  40.2 1.2 fusion.25
  41.4 0.1 fusion.51
  41.5 0.1 fusion.49
  41.6 1.4 reshape.357
  43.0 1.1 add_convert_fusion
  44.1 0.1 reshape.358
  44.2 0.1 copy.41
  44.3 0.1 copy.40
  44.4 3.3 maximum_bitcast_fusion.2
  47.7 0.4 convolution_bitcast_fusion
  48.1 0.1 fusion.31
  48.2 1.6 fusion.9
  49.8 0.0 copy-start.1
  49.8 7.6 %copy.57 = bf16[1,2,4,2,4,1024]{2,3,5,4,1,0:T(2,128)(2,1)} copy(bf16[1,2,4,2,4,1024]{5,4,2,1,3,0:T(4,128)(2,1)S(1)} %fusion.9) | data formatting | bytes 262144 | tf_op jit(solution)/shard_map/convert_element_type | solution.py:64
  57.4 0.0 copy-done.1
  57.4 35.6 %gather_fusion = bf16[4096,2,4,2]{2,3,1,0:T(2,128)(2,1)} fusion(bf16[2,4,2,4096]{1,2,3,0:T(2,128)(2,1)} %bitcast.90, s32[4096]{0:T(1024)S(1)} %broadcast_clamp_fusion), kind=kCustom, calls=%fused_computation | custom fusion | bytes 278528 | tf_op jit(solution)/shard_map/jit(_take)/gather | solution.py:79
  93.0 8.9 %copy.45 = bf16[4096,2,4,2]{0,2,3,1:T(4,128)(2,1)S(1)} copy(bf16[4096,2,4,2]{2,3,1,0:T(2,128)(2,1)} %gather_fusion) | data formatting | bytes 262144 | tf_op jit(solution)/shard_map/jit(_take)/gather | solution.py:79
  102.6 0.1 fusion.26
  102.7 0.0 copy-start
  102.7 7.3 %copy.46 = bf16[1,2,4,2,4096]{2,3,1,0,4:T(2,128)(2,1)} copy(bf16[1,2,4,2,4096]{4,2,3,1,0:T(4,128)(2,1)S(1)} %fusion.26) | data formatting | bytes 262144 | tf_op jit(solution)/shard_map/mul | solution.py:79
  110.0 9.3 %reshape.431 = bf16[32,2,1024]{2,1,0:T(2,128)(2,1)} reshape(bf16[4096,1,2,2,4]{4,3,2,1,0:T(2,128)(2,1)} %bitcast.88) | data formatting | bytes 262144
  119.3 16.0 %all-to-all-start = ((bf16[32,2,1024]{2,1,0:T(2,128)(2,1)}), bf16[32,2,1024]{2,1,0:T(2,128)(2,1)S(1)}, u32[]{:S(2)}, u32[]{:S(2)}) async-start(bf16[32,2,1024]{2,1,0:T(2,128)(2,1)} %reshape.431), calls=%async_computation | async-start | bytes 262144 | tf_op jit(solution)/shard_map/all_to_all | solution.py:82
  135.3 0.2 all-reduce.3.cloned.1.call-start
  135.5 0.0 copy-done
  135.6 3.8 %fusion.54 = (bf16[32,128,1,128]{3,2,1,0:T(2,128)(2,1)S(1)}, bf16[32,128,1,128]{3,2,1,0:T(2,128)(2,1)S(1)}) fusion(bf16[32,128,2,128]{3,2,1,0:T(2,128)(2,1)S(1)} %copy-done), kind=kLoop, calls=%fused_computation.104 | loop fusion | bytes 4194304 | tf_op jit(solution)/shard_map/jit(_take) | solution.py:69
  139.4 0.3 fusion.10
  139.7 0.2 copy.59
  139.8 0.4 maximum_bitcast_fusion.5
  140.2 0.4 maximum_bitcast_fusion.4
  140.6 6.3 %copy.50 = bf16[128,2,32,2,128]{4,3,2,1,0:T(2,128)(2,1)} copy(bf16[128,2,32,2,128]{4,0,2,3,1:T(8,128)(2,1)S(1)} %maximum_bitcast_fusion.4) | data formatting | bytes 8388608 | tf_op jit(solution)/shard_map/transpose | solution.py:89
  146.9 7.6 %reshape_reshape.3 = bf16[128,64,256]{2,1,0:T(8,128)(2,1)} reshape(bf16[128,2,32,2,128]{4,3,2,1,0:T(2,128)(2,1)} %copy.50) | data formatting | bytes 8388608 | tf_op jit(solution)/shard_map/reshape;reshape | solution.py:91
  154.5 0.0 all-to-all-done
  154.5 10.0 %reshape.432 = bf16[4096,1,2,2,4]{4,3,2,1,0:T(2,128)(2,1)} reshape(bf16[32,2,1024]{2,1,0:T(2,128)(2,1)S(1)} %all-to-all-done) | data formatting | bytes 262144
  164.5 6.1 %copy.58 = bf16[1,2,4,2,32,128]{5,4,3,2,1,0:T(8,128)(2,1)S(1)} copy(bf16[1,2,4,2,32,128]{2,3,1,5,4,0:T(2,128)(2,1)} %bitcast.89) | data formatting | bytes 262144 | tf_op jit(solution)/shard_map/all_to_all | solution.py:82
  170.6 0.2 copy.51
  170.8 2.8 convolution_convert_fusion
  173.6 0.1 convert_element_type.250
  173.8 1.3 copy.52
  175.1 0.0 all-reduce.3.cloned.1.call-update
  175.1 1.3 dynamic-slice.8
  177.0 165.3 %all-reduce.3.cloned.1.call-done = bf16[128,2,2,4,128]{4,3,2,1,0:T(4,128)(2,1)} async-done(((bf16[128,2,2,4,128]{4,3,2,1,0:T(4,128)(2,1)}), bf16[128,2,2,4,128]{4,3,2,1,0:T(4,128)(2,1)}) %all-reduce.3.cloned.1.call-update) | async-done | bytes 524304
  342.3 1.4 dynamic-slice_convert_fusion
  (4 shorter events, 0.1 us)
Async XLA Ops:
  49.8 7.6 %copy-start.1 = (s32[4096]{0:T(1024)S(1)}, s32[4096]{0:T(1024)}, u32[]{:S(2)}) copy-start(s32[4096]{0:T(1024)} %param.10) | copy-start | bytes 49156
  102.7 32.9 %copy-start = (bf16[32,128,2,128]{3,2,1,0:T(2,128)(2,1)S(1)}, bf16[32,128,2,128]{3,2,1,0:T(2,128)(2,1)}, u32[]{:S(2)}) copy-start(bf16[32,128,2,128]{3,2,1,0:T(2,128)(2,1)} %param.9) | copy-start | bytes 6291460
  119.3 35.1 %all-to-all-start = ((bf16[32,2,1024]{2,1,0:T(2,128)(2,1)}), bf16[32,2,1024]{2,1,0:T(2,128)(2,1)S(1)}, u32[]{:S(2)}, u32[]{:S(2)}) async-start(bf16[32,2,1024]{2,1,0:T(2,128)(2,1)} %reshape.431), calls=%async_computation | async-start | bytes 262144 | tf_op jit(solution)/shard_map/all_to_all | solution.py:82
  135.3 207.0 %all-reduce.3.cloned.1.call-start = ((), (), s32[]{:S(2)}) async-start(), calls=%async_computation.1 | async-start | bytes 1048576
Sparse Core Ops, SparseCore 0:
  175.2 167.0 all-reduce.2
where the time goes:
time: 351 us
  waiting for transfers between devices  165 us (47%)
  local copies, waits for them, and re-layouts  107 us (30%)
  other arithmetic  42 us (12%)
  starting transfers between devices  16.2 us (5%)
  between operations  14.9 us (4%)
  matrix products  4.84 us (1%)
    unnamed x2, waiting for transfers between devices  165 us
    gather x2, local copies, waits for them, and re-layouts, shards(): jnp.take(spectra, slot_index, axis=4)  44.5 us
    unnamed x8, local copies, waits for them, and re-layouts  20.8 us
    convert_element_type x1, other arithmetic, section_table(): sine = jnp.sin(angle).astype(dtype)  17.7 us
    all_to_all x1, starting transfers between devices, shards(): lax.all_to_all(spectra, 'chan', split_axis=4, concat_axis=0, tiled=True)  16 us
    neg x2, other arithmetic, section_table(): -sine  15.9 us
    convert_element_type x1, local copies, waits for them, and re-layouts, channelize(): spectra.reshape(stations, POLS, SPECTRA, 2, CHANNELS).astype(jnp.bfloat16)  7.59 us
    another operation x1, local copies, waits for them, and re-layouts, shards(): chosen.reshape(slot_width, 2 * group_size, 2 * (BEAMS // group_count * la...  7.58 us
  transfers between devices with their start and end apart: 2, of which 1 were waited for; matrix products, arithmetic and copies ran while one was open for 6% of the time, Pallas kernels for 0%

commit v1 on v0

v1 whole, which is shorter than its diff:
```python
import functools

import jax
import jax.numpy as jnp
import numpy as np
from jax import lax
from jax.experimental import pallas as pl
from jax.experimental.pallas import tpu as pltpu
from jax.sharding import PartitionSpec as P

CHANNELS = 4096
TAPS = 16
BEAMS = 128
POLS = 2
SPECTRA = 4
FRAMES = SPECTRA + TAPS - 1
LANES = 128
FIRST = CHANNELS // LANES
ROWS = 2 * FIRST
PARTS = 2 * POLS * SPECTRA
HALF = FIRST // 2
WIDE = 8


def tap_rows():
    total = TAPS * CHANNELS
    place = np.arange(total, dtype=np.float64)
    window = 0.54 - 0.46 * np.cos(2.0 * np.pi * place / total)
    taps = window * np.sinc((place - total // 2) / CHANNELS) / np.sqrt(CHANNELS)
    taps = taps.reshape(TAPS, FIRST, 1, LANES)
    return np.broadcast_to(taps, (TAPS, FIRST, 2, LANES)).reshape(TAPS, ROWS, LANES)


def first_matrix():
    k, q = np.arange(FIRST)[:, None], np.arange(FIRST)[None, :]
    angle = 2.0 * np.pi * (k * q % FIRST) / FIRST
    cosine, sine = np.cos(angle), np.sin(angle)
    real = np.stack([cosine, sine], 2).reshape(FIRST, ROWS)
    imag = np.stack([-sine, cosine], 2).reshape(FIRST, ROWS)
    whole = np.concatenate([real, imag], 0)
    high = whole.astype(jnp.bfloat16)
    low = (whole - high.astype(np.float64)).astype(jnp.bfloat16)
    return np.concatenate([high, low], 1)


def twiddles():
    k, n = np.arange(FIRST)[:, None], np.arange(LANES)[None, :]
    angle = 2.0 * np.pi * (k * n) / CHANNELS
    return np.stack([np.cos(angle), np.sin(angle)], 0).astype(np.float32)


def second_matrix():
    n, m = np.arange(LANES)[:, None], np.arange(LANES)[None, :]
    angle = 2.0 * np.pi * (n * m % LANES) / LANES
    cosine, sine = np.cos(angle), np.sin(angle)
    return np.block([[cosine, -sine], [sine, cosine]]).astype(jnp.bfloat16)


def spread_matrix(stations):
    out = np.zeros((POLS, 2, stations, 2, POLS, stations, WIDE, 2), np.float32)
    for p in range(POLS):
        for st in range(stations):
            out[p, 0, st, 0, p, st, :, 0] = 1.0
            out[p, 1, st, 0, p, st, :, 1] = -1.0
            out[p, 1, st, 1, p, st, :, 0] = 1.0
            out[p, 0, st, 1, p, st, :, 1] = 1.0
    return out.reshape(POLS * 2 * stations, 4 * stations * WIDE * 2).astype(jnp.bfloat16)


def channel_kernel(v_ref, owner_ref, live_ref, taps_ref, first_ref, turn_ref, second_ref, out_ref, folded_ref):
    f32, bf16 = jnp.float32, jnp.bfloat16
    step = 16
    filtered = [[None] * (ROWS // step) for _ in range(POLS * SPECTRA)]
    for p in range(POLS):
        for c in range(ROWS // step):
            sums = [None] * SPECTRA
            for u in range(FRAMES):
                x = v_ref[p, u * ROWS + c * step : u * ROWS + (c + 1) * step, :].astype(f32)
                for s in range(SPECTRA):
                    t = u - s
                    if 0 <= t < TAPS:
                        term = x * taps_ref[t, c * step : (c + 1) * step, :]
                        sums[s] = term if sums[s] is None else sums[s] + term
            for s in range(SPECTRA):
                filtered[p * SPECTRA + s][c] = sums[s].astype(bf16)
    columns = jnp.concatenate([jnp.concatenate(rows, 0) for rows in filtered], 1)
    first = jnp.dot(
        first_ref[...], jnp.concatenate([columns, columns], 0), preferred_element_type=f32
    )
    cosine, sine = turn_ref[0], turn_ref[1]
    count = POLS * SPECTRA
    for i in range(count):
        real = first[:FIRST, i * LANES : (i + 1) * LANES]
        imag = first[FIRST:, i * LANES : (i + 1) * LANES]
        folded_ref[0, pl.ds(i, FIRST, stride=count), :] = real * cosine + imag * sine
        folded_ref[1, pl.ds(i, FIRST, stride=count), :] = imag * cosine - real * sine
    folded = jnp.concatenate([folded_ref[0], folded_ref[1]], 1).astype(bf16)
    spectrum = jnp.dot(folded, second_ref[...], preferred_element_type=f32)
    spectrum = spectrum.astype(bf16).astype(f32) * live_ref[0].astype(f32)
    cut = HALF * count
    table = jnp.concatenate(
        [
            jnp.concatenate([spectrum[:cut, :LANES], spectrum[cut:, :LANES]], 1),
            jnp.concatenate([spectrum[:cut, LANES:], spectrum[cut:, LANES:]], 1),
        ],
        0,
    ).astype(bf16)
    rows = lax.broadcasted_iota(jnp.int32, (2 * LANES, LANES), 0)
    for c in range(out_ref.shape[0] // 2):
        picks = []
        lows = []
        for d in range(2):
            owner = owner_ref[2 * c + d : 2 * c + d + 1, :]
            key = ((owner >> 4) & 1) * LANES + (owner >> 5)
            picks.append(jnp.where(rows == key, 1.0, 0.0).astype(bf16))
            lows.append(jnp.broadcast_to(owner & 15, (count, LANES)))
        found = jnp.dot(table, jnp.concatenate(picks, 1), preferred_element_type=f32)
        for d in range(2):
            parts = []
            for r in range(2):
                block = found[r * cut : (r + 1) * cut, d * LANES : (d + 1) * LANES]
                total = block[:count]
                for h in range(1, HALF):
                    total = jnp.where(lows[d] == h, block[h * count : (h + 1) * count], total)
                parts.append(total)
            out_ref[2 * c + d] = jnp.concatenate(parts, 0).astype(bf16)


def channelize(volts, owner_table, live):
    volts = volts.reshape(POLS, 2, FRAMES * FIRST, LANES)
    volts = jnp.transpose(volts, (0, 2, 1, 3)).reshape(POLS, FRAMES * ROWS, LANES)
    owner = owner_table.reshape(CHANNELS // LANES, LANES)
    vmem = pl.BlockSpec(memory_space=pltpu.VMEM)
    return pl.pallas_call(
        channel_kernel,
        out_shape=jax.ShapeDtypeStruct((CHANNELS // LANES, PARTS, LANES), jnp.bfloat16),
        in_specs=[vmem, vmem, pl.BlockSpec(memory_space=pltpu.SMEM)] + [vmem] * 4,
        out_specs=vmem,
        scratch_shapes=[pltpu.VMEM((2, FIRST * POLS * SPECTRA, LANES), jnp.float32)],
        compiler_params=pltpu.CompilerParams(vmem_limit_bytes=24 * 2**20),
        name="channelize",
    )(
        volts,
        owner,
        live,
        jnp.asarray(tap_rows(), jnp.float32),
        jnp.asarray(first_matrix()),
        jnp.asarray(twiddles()),
        jnp.asarray(second_matrix()),
    )


def beam_kernel(x_ref, w_hbm, spread_ref, out_ref, w_ref, wide_ref, sem):
    f32, bf16 = jnp.float32, jnp.bfloat16
    stations = x_ref.shape[0]
    groups = LANES // WIDE
    copies = []
    for g in range(groups):
        here = pl.ds(g * 2 * WIDE, 2 * WIDE)
        copies.append(pltpu.make_async_copy(w_hbm.at[:, here, :], w_ref.at[g], sem.at[g]))
        copies[-1].start()
    wide_ref[...] = x_ref[...].reshape(stations * PARTS, LANES).astype(f32)
    turned = []
    for s in range(SPECTRA):
        rows = []
        for p in range(POLS):
            for r in range(2):
                start = r * POLS * SPECTRA + p * SPECTRA + s
                rows.append(wide_ref[pl.ds(start, stations, stride=PARTS), :])
        turned.append(jnp.concatenate(rows, 0).T)
    depth = stations * WIDE * 2
    row_slot = lax.broadcasted_iota(jnp.int32, (SPECTRA * WIDE, depth), 0) % WIDE
    column_slot = lax.broadcasted_iota(jnp.int32, (SPECTRA * WIDE, depth), 1) // 2 % WIDE
    meets = row_slot == column_slot
    together = 4
    height = SPECTRA * WIDE
    for batch in range(groups // together):
        small = []
        for g in range(batch * together, (batch + 1) * together):
            for s in range(SPECTRA):
                small.append(turned[s][g * WIDE : (g + 1) * WIDE])
        spread = jnp.dot(
            jnp.concatenate(small, 0).astype(bf16), spread_ref[...], preferred_element_type=f32
        )
        beams = []
        for i in range(together):
            g = batch * together + i
            lhs = jnp.concatenate(
                [
                    jnp.where(
                        meets,
                        spread[i * height : (i + 1) * height, b * depth : (b + 1) * depth],
                        0.0,
                    ).astype(bf16)
                    for b in range(2 * POLS)
                ],
                0,
            )
            copies[g].wait()
            product = jnp.dot(
                lhs, w_ref[g].reshape(depth, BEAMS), preferred_element_type=f32
            )
            beams.append(product.T)
        for pair in range(together // 2):
            where = (batch * together // 2 + pair) * 16
            for b in range(out_ref.shape[0]):
                out_ref[b, where : where + 16, :] = jnp.concatenate(
                    [beams[2 * pair + d][8 * b : 8 * b + 8] for d in range(2)], 0
                ).astype(bf16)


def beamform(spectra, weights):
    stations = weights.shape[0]
    groups = LANES // WIDE
    vmem = pl.BlockSpec(memory_space=pltpu.VMEM)
    weights = weights.reshape(stations, LANES * 2, BEAMS)
    return pl.pallas_call(
        beam_kernel,
        out_shape=jax.ShapeDtypeStruct((BEAMS // 8, 8 * groups, LANES), jnp.bfloat16),
        in_specs=[vmem, pl.BlockSpec(memory_space=pl.ANY), vmem],
        out_specs=vmem,
        scratch_shapes=[
            pltpu.VMEM((groups, stations, 2 * WIDE, BEAMS), jnp.bfloat16),
            pltpu.VMEM((stations * PARTS, LANES), jnp.float32),
            pltpu.SemaphoreType.DMA((groups,)),
        ],
        compiler_params=pltpu.CompilerParams(vmem_limit_bytes=24 * 2**20),
        name="beamform",
    )(spectra, weights, jnp.asarray(spread_matrix(stations)))


def sum_kernel(x_ref, out_ref):
    f32 = jnp.float32
    groups = LANES // WIDE
    held = []
    for g in range(0, groups, 2):
        total = x_ref[0, 8 * g : 8 * g + 16, :].astype(f32)
        for source in range(1, x_ref.shape[0]):
            total = total + x_ref[source, 8 * g : 8 * g + 16, :].astype(f32)
        held += [total[:8], total[8:]]
    block = lax.broadcasted_iota(jnp.int32, (8, LANES), 1) // WIDE
    bit = 1
    while bit < groups:
        upper = (block & bit) != 0
        for i in range(groups):
            if i & bit:
                continue
            low, high = held[i], held[i | bit]
            held[i] = jnp.where(upper, pltpu.roll(high, WIDE * bit, 1), low)
            held[i | bit] = jnp.where(upper, high, pltpu.roll(low, LANES - WIDE * bit, 1))
        bit *= 2
    for i in range(groups):
        r, p, s = i // (POLS * SPECTRA), i // SPECTRA % POLS, i % SPECTRA
        out_ref[:, r, p, s, :] = held[i]


def total(parts):
    vmem = pl.BlockSpec(memory_space=pltpu.VMEM)
    return pl.pallas_call(
        sum_kernel,
        out_shape=jax.ShapeDtypeStruct((8, 2, POLS, SPECTRA, LANES), jnp.float32),
        in_specs=[vmem],
        out_specs=vmem,
        name="sum_groups",
    )(parts)


def shards(voltages, beam_weights, owner_table, live_stations):
    spectra = channelize(voltages, owner_table, live_stations)
    turned = lax.all_to_all(spectra, "chan", split_axis=0, concat_axis=0, tiled=True)
    partial = beamform(turned, beam_weights)
    gathered = lax.all_to_all(partial, "grp", split_axis=0, concat_axis=0, tiled=True)
    return total(gathered)


def solution(mesh):
    in_specs = (
        P(("grp", "chan"), None, None, None),
        P("grp", "chan", None, None),
        P(),
        P(("grp", "chan")),
    )
    out_specs = P("grp", None, None, None, "chan")
    return jax.shard_map(shards, mesh=mesh, in_specs=in_specs, out_specs=out_specs, check_vma=False)
```

time: 351 us -> 65.9 us (0.19)
  the two profiles are of different devices: /device:TPU:2 before, /device:TPU:8 now
where the time goes in v1:
time: 65.9 us; the launch traced here: 65.3 us
  blocking collectives  49.3 us (75%)
  Pallas kernels  8.58 us (13%)
  local copies, waits for them, and re-layouts  6.8 us (10%)
  between operations  0.68 us (1%)
    all_to_all x1, blocking collectives, shards(): lax.all_to_all(spectra, 'chan', split_axis=0, concat_axis=0, tiled=True)  29.3 us
    all_to_all x1, blocking collectives, shards(): lax.all_to_all(partial, 'grp', split_axis=0, concat_axis=0, tiled=True)  20 us
    unnamed x16, local copies, waits for them, and re-layouts  6.8 us
    pallas_call x1, Pallas kernels, beamform(): pl.pallas_call(beam_kernel, out_shape=jax.ShapeDtypeStruct((BEAMS // 8, 8...  4.99 us
    pallas_call x1, Pallas kernels, total(): pl.pallas_call(sum_kernel, out_shape=jax.ShapeDtypeStruct((8, 2, POLS, SP...  2.04 us
    pallas_call x1, Pallas kernels, channelize(): pl.pallas_call(channel_kernel, out_shape=jax.ShapeDtypeStruct((CHANNELS /...  1.55 us

profile of v1, /device:TPU:8, one launch (start us, length us, event | category | flops | bytes accessed | tf_op | source)
XLA Modules:
  0.0 65.3 jit_solution(13921282599740713951)
XLA Ops:
  0.7 0.0 copy-start.1
  0.7 1.1 %copy-done.1 = bf16[1,2,2,77824]{3,2,1,0:T(2,128)(2,1)S(1)} copy-done((bf16[1,2,2,77824]{3,2,1,0:T(2,128)(2,1)S(1)}, bf16[1,2,2,77824]{3,2,1,0:T(2,128)(2,1)}, u32[]{:S(2)}) %copy-start.1) | copy-done | bytes 622616
  1.7 0.0 copy-start.3
  1.7 1.0 %copy-done.3 = f32[16,64,128]{2,1,0:T(8,128)S(1)} copy-done((f32[16,64,128]{2,1,0:T(8,128)S(1)}, f32[16,64,128]{2,1,0:T(8,128)}, u32[]{:S(2)}) %copy-start.3) | copy-done | bytes 524312
  2.8 0.0 copy-start.4
  2.8 0.9 %copy-done.4 = bf16[256,256]{1,0:T(8,128)(2,1)S(1)} copy-done((bf16[256,256]{1,0:T(8,128)(2,1)S(1)}, bf16[256,256]{1,0:T(8,128)(2,1)}, u32[]{:S(2)}) %copy-start.4) | copy-done | bytes 131096
  3.7 0.0 copy-start.5
  3.7 0.8 %copy-done.5 = f32[2,32,128]{2,1,0:T(8,128)S(1)} copy-done((f32[2,32,128]{2,1,0:T(8,128)S(1)}, f32[2,32,128]{2,1,0:T(8,128)}, u32[]{:S(2)}) %copy-start.5) | copy-done | bytes 32792
  4.4 0.0 copy-start.6
  4.4 0.7 %copy-done.6 = s32[4096]{0:T(1024)S(1)} copy-done((s32[4096]{0:T(1024)S(1)}, s32[4096]{0:T(1024)}, u32[]{:S(2)}) %copy-start.6) | copy-done | bytes 16408
  5.2 0.0 copy-start.7
  5.2 0.7 %copy-done.7 = bf16[64,128]{1,0:T(8,128)(2,1)S(1)} copy-done((bf16[64,128]{1,0:T(8,128)(2,1)S(1)}, bf16[64,128]{1,0:T(8,128)(2,1)}, u32[]{:S(2)}) %copy-start.7) | copy-done | bytes 16408
  5.9 0.0 copy-start.2
  5.9 1.5 %channelize.1 = bf16[32,16,128]{2,1,0:T(8,128)(2,1)S(1)} custom-call(bf16[2,1216,128]{2,1,0:T(8,128)(2,1)S(1)} %bitcast.8, s32[32,128]{1,0:T(8,128)S(1)} %bitcast.9, s32[1]{0:T(128)S(6)} %copy.11.live_ref, f32[16,64,128]{2,1,0:T(8,128)S(1)} %copy-done.3, bf16[64,128]{1,0:T(8,128)(2,1)S(1)} %copy-done.7, f32[2,32,128]{2,1,0:T(8,128)S(1)} %copy-done.5, ...), custom_call_target="tpu_custom_call" | custom-call | tf_op jit(solution)/shard_map/channelize/pallas_call | solution.py:134
  7.4 29.3 %all_to_all.10.x_ref = bf16[32,16,128]{2,1,0:T(8,128)(2,1)S(1)} all-to-all(bf16[32,16,128]{2,1,0:T(8,128)(2,1)S(1)} %channelize.1), channel_id=1, replica_groups=mesh['grp'=16,'chan'=32] {'chan'}, dimensions={0} | all-to-all | bytes 262144 | tf_op jit(solution)/shard_map/all_to_all | solution.py:270
  36.7 0.0 copy-done.2
  36.7 0.0 copy-start
  36.7 1.6 %copy-done = bf16[32,128,2,128]{3,2,1,0:T(2,128)(2,1)S(1)} copy-done((bf16[32,128,2,128]{3,2,1,0:T(2,128)(2,1)S(1)}, bf16[32,128,2,128]{3,2,1,0:T(2,128)(2,1)}, u32[]{:S(2)}) %copy-start) | copy-done | bytes 2097176
  38.3 5.0 %beamform.1 = bf16[16,128,128]{2,1,0:T(8,128)(2,1)S(1)} custom-call(bf16[32,16,128]{2,1,0:T(8,128)(2,1)S(1)} %all_to_all.10.x_ref, bf16[32,256,128]{2,1,0:T(8,128)(2,1)S(1)} %bitcast.7, bf16[128,2048]{1,0:T(8,128)(2,1)S(1)} %copy-done.2), custom_call_target="tpu_custom_call" | custom-call | tf_op jit(solution)/shard_map/beamform/pallas_call | solution.py:217
  43.3 20.0 %all_to_all.11.x_ref = bf16[16,128,128]{2,1,0:T(8,128)(2,1)} all-to-all(bf16[16,128,128]{2,1,0:T(8,128)(2,1)S(1)} %beamform.1), channel_id=1, replica_groups=mesh['grp'=16,'chan'=32] {'grp'}, dimensions={0} | all-to-all | bytes 1048576 | tf_op jit(solution)/shard_map/all_to_all | solution.py:272
  63.3 2.0 %sum_groups.1 = f32[8,2,2,4,128]{4,3,2,1,0:T(4,128)} custom-call(bf16[16,128,128]{2,1,0:T(8,128)(2,1)} %all_to_all.11.x_ref), custom_call_target="tpu_custom_call" | custom-call | tf_op jit(solution)/shard_map/sum_groups/pallas_call | solution.py:259
Async XLA Ops:
  0.7 1.1 %copy-start.1 = (bf16[1,2,2,77824]{3,2,1,0:T(2,128)(2,1)S(1)}, bf16[1,2,2,77824]{3,2,1,0:T(2,128)(2,1)}, u32[]{:S(2)}) copy-start(bf16[1,2,2,77824]{3,2,1,0:T(2,128)(2,1)} %param.9) | copy-start | bytes 1867780
  1.7 1.0 %copy-start.3 = (f32[16,64,128]{2,1,0:T(8,128)S(1)}, f32[16,64,128]{2,1,0:T(8,128)}, u32[]{:S(2)}) copy-start(f32[16,64,128]{2,1,0:T(8,128)} %constant.10.clone.taps_ref) | copy-start | bytes 1572868
  2.8 0.9 %copy-start.4 = (bf16[256,256]{1,0:T(8,128)(2,1)S(1)}, bf16[256,256]{1,0:T(8,128)(2,1)}, u32[]{:S(2)}) copy-start(bf16[256,256]{1,0:T(8,128)(2,1)} %constant.13.clone.second_ref) | copy-start | bytes 393220
  3.7 0.8 %copy-start.5 = (f32[2,32,128]{2,1,0:T(8,128)S(1)}, f32[2,32,128]{2,1,0:T(8,128)}, u32[]{:S(2)}) copy-start(f32[2,32,128]{2,1,0:T(8,128)} %constant.12.clone.turn_ref) | copy-start | bytes 98308
  4.4 0.7 %copy-start.6 = (s32[4096]{0:T(1024)S(1)}, s32[4096]{0:T(1024)}, u32[]{:S(2)}) copy-start(s32[4096]{0:T(1024)} %param.11) | copy-start | bytes 49156
  5.2 0.7 %copy-start.7 = (bf16[64,128]{1,0:T(8,128)(2,1)S(1)}, bf16[64,128]{1,0:T(8,128)(2,1)}, u32[]{:S(2)}) copy-start(bf16[64,128]{1,0:T(8,128)(2,1)} %constant.11.clone.first_ref) | copy-start | bytes 49156
  5.9 30.8 %copy-start.2 = (bf16[128,2048]{1,0:T(8,128)(2,1)S(1)}, bf16[128,2048]{1,0:T(8,128)(2,1)}, u32[]{:S(2)}) copy-start(bf16[128,2048]{1,0:T(8,128)(2,1)} %constant.14.clone.spread_ref) | copy-start | bytes 1572868
  36.7 1.6 %copy-start = (bf16[32,128,2,128]{3,2,1,0:T(2,128)(2,1)S(1)}, bf16[32,128,2,128]{3,2,1,0:T(2,128)(2,1)}, u32[]{:S(2)}) copy-start(bf16[32,128,2,128]{3,2,1,0:T(2,128)(2,1)} %param.10) | copy-start | bytes 6291460

commit v2 on v1

--- a/solution.py
+++ b/solution.py
@@ -67,11 +67,59 @@
     return out.reshape(POLS * 2 * stations, 4 * stations * WIDE * 2).astype(jnp.bfloat16)
 
 
-def channel_kernel(v_ref, owner_ref, live_ref, taps_ref, first_ref, turn_ref, second_ref, out_ref, folded_ref):
+def channel_kernel(
+    v_hbm,
+    owner_hbm,
+    live_ref,
+    taps_hbm,
+    first_hbm,
+    turn_hbm,
+    second_hbm,
+    w_hbm,
+    spread_hbm,
+    out_ref,
+    w_ref,
+    spread_ref,
+    v_ref,
+    owner_ref,
+    taps_ref,
+    first_ref,
+    turn_ref,
+    second_ref,
+    pick_ref,
+    folded_ref,
+    sem,
+):
     f32, bf16 = jnp.float32, jnp.bfloat16
+    pairs = [
+        (owner_hbm, owner_ref),
+        (taps_hbm, taps_ref),
+        (v_hbm.at[0], v_ref.at[0]),
+        (v_hbm.at[1], v_ref.at[1]),
+        (first_hbm, first_ref),
+        (turn_hbm, turn_ref),
+        (second_hbm, second_ref),
+        (spread_hbm, spread_ref),
+        (w_hbm, w_ref),
+    ]
+    copies = [pltpu.make_async_copy(a, b, sem.at[i]) for i, (a, b) in enumerate(pairs)]
+    for copy in copies:
+        copy.start()
+    blocks = out_ref.shape[0]
+    count = POLS * SPECTRA
+
+    copies[0].wait()
+    rows = lax.broadcasted_iota(jnp.int32, (2 * LANES, LANES), 0)
+    for c in range(blocks):
+        owner = owner_ref[c : c + 1, :]
+        key = ((owner >> 4) & 1) * LANES + (owner >> 5)
+        pick_ref[:, c * LANES : (c + 1) * LANES] = jnp.where(rows == key, 1.0, 0.0).astype(bf16)
+
+    copies[1].wait()
     step = 16
-    filtered = [[None] * (ROWS // step) for _ in range(POLS * SPECTRA)]
+    filtered = [[None] * (ROWS // step) for _ in range(count)]
     for p in range(POLS):
+        copies[2 + p].wait()
         for c in range(ROWS // step):
             sums = [None] * SPECTRA
             for u in range(FRAMES):
@@ -84,17 +132,19 @@
             for s in range(SPECTRA):
                 filtered[p * SPECTRA + s][c] = sums[s].astype(bf16)
     columns = jnp.concatenate([jnp.concatenate(rows, 0) for rows in filtered], 1)
+    copies[4].wait()
     first = jnp.dot(
         first_ref[...], jnp.concatenate([columns, columns], 0), preferred_element_type=f32
     )
+    copies[5].wait()
     cosine, sine = turn_ref[0], turn_ref[1]
-    count = POLS * SPECTRA
     for i in range(count):
         real = first[:FIRST, i * LANES : (i + 1) * LANES]
         imag = first[FIRST:, i * LANES : (i + 1) * LANES]
         folded_ref[0, pl.ds(i, FIRST, stride=count), :] = real * cosine + imag * sine
         folded_ref[1, pl.ds(i, FIRST, stride=count), :] = imag * cosine - real * sine
     folded = jnp.concatenate([folded_ref[0], folded_ref[1]], 1).astype(bf16)
+    copies[6].wait()
     spectrum = jnp.dot(folded, second_ref[...], preferred_element_type=f32)
     spectrum = spectrum.astype(bf16).astype(f32) * live_ref[0].astype(f32)
     cut = HALF * count
@@ -105,60 +155,68 @@
         ],
         0,
     ).astype(bf16)
-    rows = lax.broadcasted_iota(jnp.int32, (2 * LANES, LANES), 0)
-    for c in range(out_ref.shape[0] // 2):
-        picks = []
-        lows = []
+    for c in range(0, blocks, 2):
+        found = jnp.dot(
+            table, pick_ref[:, c * LANES : (c + 2) * LANES], preferred_element_type=f32
+        )
         for d in range(2):
-            owner = owner_ref[2 * c + d : 2 * c + d + 1, :]
-            key = ((owner >> 4) & 1) * LANES + (owner >> 5)
-            picks.append(jnp.where(rows == key, 1.0, 0.0).astype(bf16))
-            lows.append(jnp.broadcast_to(owner & 15, (count, LANES)))
-        found = jnp.dot(table, jnp.concatenate(picks, 1), preferred_element_type=f32)
-        for d in range(2):
+            low = jnp.broadcast_to(owner_ref[c + d : c + d + 1, :] & 15, (count, LANES))
             parts = []
             for r in range(2):
                 block = found[r * cut : (r + 1) * cut, d * LANES : (d + 1) * LANES]
                 total = block[:count]
                 for h in range(1, HALF):
-                    total = jnp.where(lows[d] == h, block[h * count : (h + 1) * count], total)
+                    total = jnp.where(low == h, block[h * count : (h + 1) * count], total)
                 parts.append(total)
-            out_ref[2 * c + d] = jnp.concatenate(parts, 0).astype(bf16)
-
-
-def channelize(volts, owner_table, live):
+            out_ref[c + d] = jnp.concatenate(parts, 0).astype(bf16)
+    copies[7].wait()
+    copies[8].wait()
+
+
+def place(array):
+    return pltpu.with_memory_space_constraint(array, pltpu.HBM)
+
+
+def channelize(volts, owner_table, live, weights):
     volts = volts.reshape(POLS, 2, FRAMES * FIRST, LANES)
     volts = jnp.transpose(volts, (0, 2, 1, 3)).reshape(POLS, FRAMES * ROWS, LANES)
     owner = owner_table.reshape(CHANNELS // LANES, LANES)
-    vmem = pl.BlockSpec(memory_space=pltpu.VMEM)
-    return pl.pallas_call(
-        channel_kernel,
-        out_shape=jax.ShapeDtypeStruct((CHANNELS // LANES, PARTS, LANES), jnp.bfloat16),
-        in_specs=[vmem, vmem, pl.BlockSpec(memory_space=pltpu.SMEM)] + [vmem] * 4,
-        out_specs=vmem,
-        scratch_shapes=[pltpu.VMEM((2, FIRST * POLS * SPECTRA, LANES), jnp.float32)],
-        compiler_params=pltpu.CompilerParams(vmem_limit_bytes=24 * 2**20),
-        name="channelize",
-    )(
-        volts,
-        owner,
-        live,
+    stations = weights.shape[0]
+    weights = weights.reshape(stations, LANES * 2, BEAMS)
+    constants = [
         jnp.asarray(tap_rows(), jnp.float32),
         jnp.asarray(first_matrix()),
         jnp.asarray(twiddles()),
         jnp.asarray(second_matrix()),
-    )
-
-
-def beam_kernel(x_ref, w_hbm, spread_ref, out_ref, w_ref, wide_ref, sem):
+    ]
+    spread = jnp.asarray(spread_matrix(stations))
+    vmem = pl.BlockSpec(memory_space=pltpu.VMEM)
+    hbm = pl.BlockSpec(memory_space=pltpu.HBM)
+    held = [pltpu.VMEM(a.shape, a.dtype) for a in [volts, owner] + constants]
+    return pl.pallas_call(
+        channel_kernel,
+        out_shape=[
+            jax.ShapeDtypeStruct((CHANNELS // LANES, PARTS, LANES), jnp.bfloat16),
+            jax.ShapeDtypeStruct(weights.shape, jnp.bfloat16),
+            jax.ShapeDtypeStruct(spread.shape, jnp.bfloat16),
+        ],
+        in_specs=[hbm, hbm, pl.BlockSpec(memory_space=pltpu.SMEM)] + [hbm] * 6,
+        out_specs=[vmem] * 3,
+        scratch_shapes=held
+        + [
+            pltpu.VMEM((2 * LANES, CHANNELS), jnp.bfloat16),
+            pltpu.VMEM((2, FIRST * POLS * SPECTRA, LANES), jnp.float32),
+            pltpu.SemaphoreType.DMA((9,)),
+        ],
+        compiler_params=pltpu.CompilerParams(vmem_limit_bytes=20 * 2**20),
+        name="channelize",
+    )(*[place(a) for a in (volts, owner)], live, *[place(a) for a in constants + [weights, spread]])
+
+
+def beam_kernel(x_ref, w_ref, spread_ref, out_ref, wide_ref):
     f32, bf16 = jnp.float32, jnp.bfloat16
     stations = x_ref.shape[0]
     groups = LANES // WIDE
-    copies = []
-    for g in range(groups):
-        here = pl.ds(g * 2 * WIDE, 2 * WIDE)
-        copies.append(pltpu.make_async_copy(w_hbm.at[:, here, :], w_ref.at[g], sem.at[g]))
-        copies[-1].start()
     wide_ref[...] = x_ref[...].reshape(stations * PARTS, LANES).astype(f32)
     turned = []
     for s in range(SPECTRA):
@@ -196,10 +254,8 @@
                 ],
                 0,
             )
-            copies[g].wait()
-            product = jnp.dot(
-                lhs, w_ref[g].reshape(depth, BEAMS), preferred_element_type=f32
-            )
+            weights = w_ref[:, g * 2 * WIDE : (g + 1) * 2 * WIDE, :].reshape(depth, BEAMS)
+            product = jnp.dot(lhs, weights, preferred_element_type=f32)
             beams.append(product.T)
         for pair in range(together // 2):
             where = (batch * together // 2 + pair) * 16
@@ -209,24 +265,19 @@
                 ).astype(bf16)
 
 
-def beamform(spectra, weights):
+def beamform(spectra, weights, spread):
     stations = weights.shape[0]
     groups = LANES // WIDE
     vmem = pl.BlockSpec(memory_space=pltpu.VMEM)
-    weights = weights.reshape(stations, LANES * 2, BEAMS)
     return pl.pallas_call(
         beam_kernel,
         out_shape=jax.ShapeDtypeStruct((BEAMS // 8, 8 * groups, LANES), jnp.bfloat16),
-        in_specs=[vmem, pl.BlockSpec(memory_space=pl.ANY), vmem],
+        in_specs=[vmem] * 3,
         out_specs=vmem,
-        scratch_shapes=[
-            pltpu.VMEM((groups, stations, 2 * WIDE, BEAMS), jnp.bfloat16),
-            pltpu.VMEM((stations * PARTS, LANES), jnp.float32),
-            pltpu.SemaphoreType.DMA((groups,)),
-        ],
-        compiler_params=pltpu.CompilerParams(vmem_limit_bytes=24 * 2**20),
+        scratch_shapes=[pltpu.VMEM((stations * PARTS, LANES), jnp.float32)],
+        compiler_params=pltpu.CompilerParams(vmem_limit_bytes=20 * 2**20),
         name="beamform",
-    )(spectra, weights, jnp.asarray(spread_matrix(stations)))
+    )(spectra, weights, spread)
 
 
 def sum_kernel(x_ref, out_ref):
@@ -261,14 +312,15 @@
         out_shape=jax.ShapeDtypeStruct((8, 2, POLS, SPECTRA, LANES), jnp.float32),
         in_specs=[vmem],
         out_specs=vmem,
+        compiler_params=pltpu.CompilerParams(vmem_limit_bytes=20 * 2**20),
         name="sum_groups",
     )(parts)
 
 
 def shards(voltages, beam_weights, owner_table, live_stations):
-    spectra = channelize(voltages, owner_table, live_stations)
+    spectra, weights, spread = channelize(voltages, owner_table, live_stations, beam_weights)
     turned = lax.all_to_all(spectra, "chan", split_axis=0, concat_axis=0, tiled=True)
-    partial = beamform(turned, beam_weights)
+    partial = beamform(turned, weights, spread)
     gathered = lax.all_to_all(partial, "grp", split_axis=0, concat_axis=0, tiled=True)
     return total(gathered)
 

time: 65.9 us -> 55.6 us (0.84)
  local copies, waits for them, and re-layouts: 6.8 us -> 0 us
  Pallas kernels: 8.58 us -> 5.55 us
    unnamed x16 -> x0, local copies, waits for them, and re-layouts: 6.8 us -> none
    pallas_call x1, Pallas kernels: 4.99 us -> 1.79 us  [beamform(): pl.pallas_call(beam_kernel, out_shape=jax.ShapeDtypeStruct((BEAMS // 8, 8...]
    pallas_call x1, Pallas kernels: 1.55 us -> 2.77 us  [channelize(): pl.pallas_call(channel_kernel, out_shape=[jax.ShapeDtypeStruct((CHANNELS...]
    pallas_call x1, Pallas kernels: 2.04 us -> 1 us  [total(): pl.pallas_call(sum_kernel, out_shape=jax.ShapeDtypeStruct((8, 2, POLS, SP...]
where the time goes in v2:
time: 55.6 us; the launch traced here: 55.4 us
  blocking collectives  49.1 us (88%)
  Pallas kernels  5.55 us (10%)
  between operations  0.67 us (1%)
    all_to_all x1, blocking collectives, shards(): lax.all_to_all(spectra, 'chan', split_axis=0, concat_axis=0, tiled=True)  29.3 us
    all_to_all x1, blocking collectives, shards(): lax.all_to_all(partial, 'grp', split_axis=0, concat_axis=0, tiled=True)  19.9 us
    pallas_call x1, Pallas kernels, channelize(): pl.pallas_call(channel_kernel, out_shape=[jax.ShapeDtypeStruct((CHANNELS...  2.77 us
    pallas_call x1, Pallas kernels, beamform(): pl.pallas_call(beam_kernel, out_shape=jax.ShapeDtypeStruct((BEAMS // 8, 8...  1.79 us

profile of v2, /device:TPU:8, one launch (start us, length us, event | category | flops | bytes accessed | tf_op | source)
XLA Modules:
  0.0 55.4 jit_solution(78907101743701078)
XLA Ops:
  0.7 2.8 %channelize.1 = (bf16[32,16,128]{2,1,0:T(8,128)(2,1)S(1)}, bf16[32,256,128]{2,1,0:T(8,128)(2,1)S(1)}, bf16[128,2048]{1,0:T(8,128)(2,1)S(1)}) custom-call(bf16[2,1216,128]{2,1,0:T(8,128)(2,1)} %bitcast.8, s32[32,128]{1,0:T(8,128)} %bitcast.9, s32[1]{0:T(128)S(6)} %copy.11.live_ref, f32[16,64,128]{2,1,0:T(8,128)} %constant.10.clone.taps_hbm, ...), custom_call_target="tpu_custom_call" | custom-call | tf_op jit(solution)/shard_map/channelize/pallas_call | solution.py:196
  3.4 29.3 %all_to_all.10.x_ref = bf16[32,16,128]{2,1,0:T(8,128)(2,1)S(1)} all-to-all(bf16[32,16,128]{2,1,0:T(8,128)(2,1)S(1)} %get-tuple-element.8), channel_id=1, replica_groups=mesh['grp'=16,'chan'=32] {'chan'}, dimensions={0} | all-to-all | bytes 262144 | tf_op jit(solution)/shard_map/all_to_all | solution.py:322
  32.7 1.8 %beamform.1 = bf16[16,128,128]{2,1,0:T(8,128)(2,1)S(1)} custom-call(bf16[32,16,128]{2,1,0:T(8,128)(2,1)S(1)} %all_to_all.10.x_ref, bf16[32,256,128]{2,1,0:T(8,128)(2,1)S(1)} %get-tuple-element.9.w_ref, bf16[128,2048]{1,0:T(8,128)(2,1)S(1)} %get-tuple-element.10.spread_ref), custom_call_target="tpu_custom_call" | custom-call | tf_op jit(solution)/shard_map/beamform/pallas_call | solution.py:272
  34.5 19.9 %all_to_all.11.x_ref = bf16[16,128,128]{2,1,0:T(8,128)(2,1)S(1)} all-to-all(bf16[16,128,128]{2,1,0:T(8,128)(2,1)S(1)} %beamform.1), channel_id=1, replica_groups=mesh['grp'=16,'chan'=32] {'grp'}, dimensions={0} | all-to-all | bytes 1048576 | tf_op jit(solution)/shard_map/all_to_all | solution.py:324
  54.4 1.0 %sum_groups.1 = f32[8,2,2,4,128]{4,3,2,1,0:T(4,128)} custom-call(bf16[16,128,128]{2,1,0:T(8,128)(2,1)S(1)} %all_to_all.11.x_ref), custom_call_target="tpu_custom_call" | custom-call | tf_op jit(solution)/shard_map/sum_groups/pallas_call | solution.py:310

commit v3 on v2

--- a/solution.py
+++ b/solution.py
@@ -20,6 +20,12 @@
 PARTS = 2 * POLS * SPECTRA
 HALF = FIRST // 2
 WIDE = 8
+CHAN_LEAD = 30
+GRP_LEAD = 10
+
+
+def leading(first, count):
+    return [first] + [i for i in range(count) if i != first]
 
 
 def tap_rows():
@@ -59,11 +65,11 @@
 def spread_matrix(stations):
     out = np.zeros((POLS, 2, stations, 2, POLS, stations, WIDE, 2), np.float32)
     for p in range(POLS):
-        for st in range(stations):
-            out[p, 0, st, 0, p, st, :, 0] = 1.0
-            out[p, 1, st, 0, p, st, :, 1] = -1.0
-            out[p, 1, st, 1, p, st, :, 0] = 1.0
-            out[p, 0, st, 1, p, st, :, 1] = 1.0
+        for i, st in enumerate(leading(CHAN_LEAD, stations)):
+            out[p, 0, i, 0, p, st, :, 0] = 1.0
+            out[p, 1, i, 0, p, st, :, 1] = -1.0
+            out[p, 1, i, 1, p, st, :, 0] = 1.0
+            out[p, 0, i, 1, p, st, :, 1] = 1.0
     return out.reshape(POLS * 2 * stations, 4 * stations * WIDE * 2).astype(jnp.bfloat16)
 
 
@@ -155,6 +161,7 @@
         ],
         0,
     ).astype(bf16)
+    place_of = {c: i for i, c in enumerate(leading(CHAN_LEAD, blocks))}
     for c in range(0, blocks, 2):
         found = jnp.dot(
             table, pick_ref[:, c * LANES : (c + 2) * LANES], preferred_element_type=f32
@@ -168,7 +175,7 @@
                 for h in range(1, HALF):
                     total = jnp.where(low == h, block[h * count : (h + 1) * count], total)
                 parts.append(total)
-            out_ref[c + d] = jnp.concatenate(parts, 0).astype(bf16)
+            out_ref[place_of[c + d]] = jnp.concatenate(parts, 0).astype(bf16)
     copies[7].wait()
     copies[8].wait()
 
@@ -259,8 +266,8 @@
             beams.append(product.T)
         for pair in range(together // 2):
             where = (batch * together // 2 + pair) * 16
-            for b in range(out_ref.shape[0]):
-                out_ref[b, where : where + 16, :] = jnp.concatenate(
+            for i, b in enumerate(leading(GRP_LEAD, out_ref.shape[0])):
+                out_ref[i, where : where + 16, :] = jnp.concatenate(
                     [beams[2 * pair + d][8 * b : 8 * b + 8] for d in range(2)], 0
                 ).astype(bf16)
 
@@ -317,11 +324,18 @@
     )(parts)
 
 
+def exchange(blocks, axis, first):
+    order = leading(first, blocks.shape[0])
+    return lax.all_to_all(
+        blocks, axis, split_axis=0, concat_axis=0, axis_index_groups=[order], tiled=True
+    )
+
+
 def shards(voltages, beam_weights, owner_table, live_stations):
     spectra, weights, spread = channelize(voltages, owner_table, live_stations, beam_weights)
-    turned = lax.all_to_all(spectra, "chan", split_axis=0, concat_axis=0, tiled=True)
+    turned = exchange(spectra, "chan", CHAN_LEAD)
     partial = beamform(turned, weights, spread)
-    gathered = lax.all_to_all(partial, "grp", split_axis=0, concat_axis=0, tiled=True)
+    gathered = exchange(partial, "grp", GRP_LEAD)
     return total(gathered)
 
 

time: 55.6 us -> 48.8 us (0.88)
  the two profiles are of different devices: /device:TPU:8 before, /device:TPU:60 now
where the time goes in v3:
time: 48.8 us; the launch traced here: 48.5 us
  blocking collectives  42.3 us (87%)
  Pallas kernels  5.54 us (11%)
  between operations  0.67 us (1%)
    all_to_all x2, blocking collectives, exchange(): lax.all_to_all(blocks, axis, split_axis=0, concat_axis=0, axis_index_grou...  42.3 us
    pallas_call x1, Pallas kernels, channelize(): pl.pallas_call(channel_kernel, out_shape=[jax.ShapeDtypeStruct((CHANNELS...  2.76 us
    pallas_call x1, Pallas kernels, beamform(): pl.pallas_call(beam_kernel, out_shape=jax.ShapeDtypeStruct((BEAMS // 8, 8...  1.79 us
    pallas_call x1, Pallas kernels, total(): pl.pallas_call(sum_kernel, out_shape=jax.ShapeDtypeStruct((8, 2, POLS, SP...  1 us

profile of v3, /device:TPU:60, one launch (start us, length us, event | category | flops | bytes accessed | tf_op | source)
XLA Modules:
  0.0 48.5 jit_solution(8328165826921772571)
XLA Ops:
  0.7 2.8 %channelize.1 = (bf16[32,16,128]{2,1,0:T(8,128)(2,1)S(1)}, bf16[32,256,128]{2,1,0:T(8,128)(2,1)S(1)}, bf16[128,2048]{1,0:T(8,128)(2,1)S(1)}) custom-call(bf16[2,1216,128]{2,1,0:T(8,128)(2,1)} %bitcast.8, s32[32,128]{1,0:T(8,128)} %bitcast.9, s32[1]{0:T(128)S(6)} %copy.11.live_ref, f32[16,64,128]{2,1,0:T(8,128)} %constant.10.clone.taps_hbm, ...), custom_call_target="tpu_custom_call" | custom-call | tf_op jit(solution)/shard_map/channelize/pallas_call | solution.py:203
  3.4 23.6 %all_to_all.10.x_ref = bf16[32,16,128]{2,1,0:T(8,128)(2,1)S(1)} all-to-all(bf16[32,16,128]{2,1,0:T(8,128)(2,1)S(1)} %get-tuple-element.8), channel_id=1, replica_groups={{30,0,1,2,3,4,5,6,7,8,9,10,11,12,13,14,15,16,17,18,19,20,21,22,23,24,25..., dimensions={0} | all-to-all | bytes 262144 | tf_op jit(solution)/shard_map/all_to_all | solution.py:329
  27.0 1.8 %beamform.1 = bf16[16,128,128]{2,1,0:T(8,128)(2,1)S(1)} custom-call(bf16[32,16,128]{2,1,0:T(8,128)(2,1)S(1)} %all_to_all.10.x_ref, bf16[32,256,128]{2,1,0:T(8,128)(2,1)S(1)} %get-tuple-element.9.w_ref, bf16[128,2048]{1,0:T(8,128)(2,1)S(1)} %get-tuple-element.10.spread_ref), custom_call_target="tpu_custom_call" | custom-call | tf_op jit(solution)/shard_map/beamform/pallas_call | solution.py:279
  28.8 18.8 %all_to_all.11.x_ref = bf16[16,128,128]{2,1,0:T(8,128)(2,1)S(1)} all-to-all(bf16[16,128,128]{2,1,0:T(8,128)(2,1)S(1)} %beamform.1), channel_id=1, replica_groups={{320,0,32,64,96,128,160,192,224,256,288,352,384,416,448,480},{321,1,33,..., dimensions={0} | all-to-all | bytes 1048576 | tf_op jit(solution)/shard_map/all_to_all | solution.py:329
  47.6 1.0 %sum_groups.1 = f32[8,2,2,4,128]{4,3,2,1,0:T(4,128)} custom-call(bf16[16,128,128]{2,1,0:T(8,128)(2,1)S(1)} %all_to_all.11.x_ref), custom_call_target="tpu_custom_call" | custom-call | tf_op jit(solution)/shard_map/sum_groups/pallas_call | solution.py:317

commit v4 on v3

--- a/solution.py
+++ b/solution.py
@@ -115,11 +115,12 @@
     count = POLS * SPECTRA
 
     copies[0].wait()
-    rows = lax.broadcasted_iota(jnp.int32, (2 * LANES, LANES), 0)
+    rows = lax.broadcasted_iota(jnp.int32, (2 * LANES, LANES), 0).astype(f32).astype(bf16)
+    one, zero = jnp.ones((), bf16), jnp.zeros((), bf16)
     for c in range(blocks):
         owner = owner_ref[c : c + 1, :]
-        key = ((owner >> 4) & 1) * LANES + (owner >> 5)
-        pick_ref[:, c * LANES : (c + 1) * LANES] = jnp.where(rows == key, 1.0, 0.0).astype(bf16)
+        key = (((owner >> 4) & 1) * LANES + (owner >> 5)).astype(f32).astype(bf16)
+        pick_ref[:, c * LANES : (c + 1) * LANES] = jnp.where(rows == key, one, zero)
 
     copies[1].wait()
     step = 16
@@ -237,7 +238,7 @@
     row_slot = lax.broadcasted_iota(jnp.int32, (SPECTRA * WIDE, depth), 0) % WIDE
     column_slot = lax.broadcasted_iota(jnp.int32, (SPECTRA * WIDE, depth), 1) // 2 % WIDE
     meets = row_slot == column_slot
-    together = 4
+    together = 16
     height = SPECTRA * WIDE
     for batch in range(groups // together):
         small = []
@@ -297,16 +298,21 @@
             total = total + x_ref[source, 8 * g : 8 * g + 16, :].astype(f32)
         held += [total[:8], total[8:]]
     block = lax.broadcasted_iota(jnp.int32, (8, LANES), 1) // WIDE
-    bit = 1
-    while bit < groups:
-        upper = (block & bit) != 0
+    radix = 4
+    for unit in (1, radix):
+        digit = block // unit % radix
+        turned = [None] * groups
         for i in range(groups):
-            if i & bit:
-                continue
-            low, high = held[i], held[i | bit]
-            held[i] = jnp.where(upper, pltpu.roll(high, WIDE * bit, 1), low)
-            held[i | bit] = jnp.where(upper, high, pltpu.roll(low, LANES - WIDE * bit, 1))
-        bit *= 2
+            mine = i // unit % radix
+            total = held[i]
+            for other in range(radix):
+                if other != mine:
+                    moved = pltpu.roll(
+                        held[i + (other - mine) * unit], (other - mine) * unit * WIDE % LANES, 1
+                    )
+                    total = jnp.where(digit == other, moved, total)
+            turned[i] = total
+        held = turned
     for i in range(groups):
         r, p, s = i // (POLS * SPECTRA), i // SPECTRA % POLS, i % SPECTRA
         out_ref[:, r, p, s, :] = held[i]

time: 48.8 us -> 48.3 us (0.990)
  no operation moved by 1% of the time
where the time goes in v4:
time: 48.3 us; the launch traced here: 48.1 us
  blocking collectives  42.3 us (88%)
  Pallas kernels  5.09 us (11%)
  between operations  0.67 us (1%)
    all_to_all x2, blocking collectives, exchange(): lax.all_to_all(blocks, axis, split_axis=0, concat_axis=0, axis_index_grou...  42.3 us
    pallas_call x1, Pallas kernels, channelize(): pl.pallas_call(channel_kernel, out_shape=[jax.ShapeDtypeStruct((CHANNELS...  2.76 us
    pallas_call x1, Pallas kernels, beamform(): pl.pallas_call(beam_kernel, out_shape=jax.ShapeDtypeStruct((BEAMS // 8, 8...  1.42 us

profile of v4, /device:TPU:60, one launch (start us, length us, event | category | flops | bytes accessed | tf_op | source)
XLA Modules:
  0.0 48.1 jit_solution(760087573070821990)
XLA Ops:
  0.7 2.8 %channelize.1 = (bf16[32,16,128]{2,1,0:T(8,128)(2,1)S(1)}, bf16[32,256,128]{2,1,0:T(8,128)(2,1)S(1)}, bf16[128,2048]{1,0:T(8,128)(2,1)S(1)}) custom-call(bf16[2,1216,128]{2,1,0:T(8,128)(2,1)} %bitcast.8, s32[32,128]{1,0:T(8,128)} %bitcast.9, s32[1]{0:T(128)S(6)} %copy.11.live_ref, f32[16,64,128]{2,1,0:T(8,128)} %constant.10.clone.taps_hbm, ...), custom_call_target="tpu_custom_call" | custom-call | tf_op jit(solution)/shard_map/channelize/pallas_call | solution.py:204
  3.4 23.6 %all_to_all.10.x_ref = bf16[32,16,128]{2,1,0:T(8,128)(2,1)S(1)} all-to-all(bf16[32,16,128]{2,1,0:T(8,128)(2,1)S(1)} %get-tuple-element.8), channel_id=1, replica_groups={{30,0,1,2,3,4,5,6,7,8,9,10,11,12,13,14,15,16,17,18,19,20,21,22,23,24,25..., dimensions={0} | all-to-all | bytes 262144 | tf_op jit(solution)/shard_map/all_to_all | solution.py:335
  27.0 1.4 %beamform.1 = bf16[16,128,128]{2,1,0:T(8,128)(2,1)S(1)} custom-call(bf16[32,16,128]{2,1,0:T(8,128)(2,1)S(1)} %all_to_all.10.x_ref, bf16[32,256,128]{2,1,0:T(8,128)(2,1)S(1)} %get-tuple-element.9.w_ref, bf16[128,2048]{1,0:T(8,128)(2,1)S(1)} %get-tuple-element.10.spread_ref), custom_call_target="tpu_custom_call" | custom-call | tf_op jit(solution)/shard_map/beamform/pallas_call | solution.py:280
  28.4 18.8 %all_to_all.11.x_ref = bf16[16,128,128]{2,1,0:T(8,128)(2,1)S(1)} all-to-all(bf16[16,128,128]{2,1,0:T(8,128)(2,1)S(1)} %beamform.1), channel_id=1, replica_groups={{320,0,32,64,96,128,160,192,224,256,288,352,384,416,448,480},{321,1,33,..., dimensions={0} | all-to-all | bytes 1048576 | tf_op jit(solution)/shard_map/all_to_all | solution.py:335
  47.2 0.9 %sum_groups.1 = f32[8,2,2,4,128]{4,3,2,1,0:T(4,128)} custom-call(bf16[16,128,128]{2,1,0:T(8,128)(2,1)S(1)} %all_to_all.11.x_ref), custom_call_target="tpu_custom_call" | custom-call | tf_op jit(solution)/shard_map/sum_groups/pallas_call | solution.py:323

commit v5 on v4

--- a/solution.py
+++ b/solution.py
@@ -78,9 +78,7 @@
     owner_hbm,
     live_ref,
     taps_hbm,
-    first_hbm,
-    turn_hbm,
-    second_hbm,
+    matrix_hbm,
     w_hbm,
     spread_hbm,
     out_ref,
@@ -89,9 +87,7 @@
     v_ref,
     owner_ref,
     taps_ref,
-    first_ref,
-    turn_ref,
-    second_ref,
+    matrix_ref,
     pick_ref,
     folded_ref,
     sem,
@@ -100,11 +96,8 @@
     pairs = [
         (owner_hbm, owner_ref),
         (taps_hbm, taps_ref),
-        (v_hbm.at[0], v_ref.at[0]),
-        (v_hbm.at[1], v_ref.at[1]),
-        (first_hbm, first_ref),
-        (turn_hbm, turn_ref),
-        (second_hbm, second_ref),
+        (v_hbm, v_ref),
+        (matrix_hbm, matrix_ref),
         (spread_hbm, spread_ref),
         (w_hbm, w_ref),
     ]
@@ -123,10 +116,10 @@
         pick_ref[:, c * LANES : (c + 1) * LANES] = jnp.where(rows == key, one, zero)
 
     copies[1].wait()
+    copies[2].wait()
     step = 16
     filtered = [[None] * (ROWS // step) for _ in range(count)]
     for p in range(POLS):
-        copies[2 + p].wait()
         for c in range(ROWS // step):
             sums = [None] * SPECTRA
             for u in range(FRAMES):
@@ -139,20 +132,19 @@
             for s in range(SPECTRA):
                 filtered[p * SPECTRA + s][c] = sums[s].astype(bf16)
     columns = jnp.concatenate([jnp.concatenate(rows, 0) for rows in filtered], 1)
-    copies[4].wait()
+    copies[3].wait()
     first = jnp.dot(
-        first_ref[...], jnp.concatenate([columns, columns], 0), preferred_element_type=f32
+        matrix_ref[:ROWS], jnp.concatenate([columns, columns], 0), preferred_element_type=f32
     )
-    copies[5].wait()
-    cosine, sine = turn_ref[0], turn_ref[1]
+    cosine, sine = taps_ref[TAPS, :FIRST], taps_ref[TAPS, FIRST:]
     for i in range(count):
         real = first[:FIRST, i * LANES : (i + 1) * LANES]
         imag = first[FIRST:, i * LANES : (i + 1) * LANES]
         folded_ref[0, pl.ds(i, FIRST, stride=count), :] = real * cosine + imag * sine
         folded_ref[1, pl.ds(i, FIRST, stride=count), :] = imag * cosine - real * sine
     folded = jnp.concatenate([folded_ref[0], folded_ref[1]], 1).astype(bf16)
-    copies[6].wait()
-    spectrum = jnp.dot(folded, second_ref[...], preferred_element_type=f32)
+    second = jnp.concatenate([matrix_ref[ROWS : 5 * LANES // 2], matrix_ref[5 * LANES // 2 :]], 1)
+    spectrum = jnp.dot(folded, second, preferred_element_type=f32)
     spectrum = spectrum.astype(bf16).astype(f32) * live_ref[0].astype(f32)
     cut = HALF * count
     table = jnp.concatenate(
@@ -177,8 +169,8 @@
                     total = jnp.where(low == h, block[h * count : (h + 1) * count], total)
                 parts.append(total)
             out_ref[place_of[c + d]] = jnp.concatenate(parts, 0).astype(bf16)
-    copies[7].wait()
-    copies[8].wait()
+    copies[4].wait()
+    copies[5].wait()
 
 
 def place(array):
@@ -191,11 +183,10 @@
     owner = owner_table.reshape(CHANNELS // LANES, LANES)
     stations = weights.shape[0]
     weights = weights.reshape(stations, LANES * 2, BEAMS)
+    second = second_matrix()
     constants = [
-        jnp.asarray(tap_rows(), jnp.float32),
-        jnp.asarray(first_matrix()),
-        jnp.asarray(twiddles()),
-        jnp.asarray(second_matrix()),
+        jnp.asarray(np.concatenate([tap_rows(), twiddles().reshape(1, ROWS, LANES)]), jnp.float32),
+        jnp.asarray(np.concatenate([first_matrix(), second[:, :LANES], second[:, LANES:]])),
     ]
     spread = jnp.asarray(spread_matrix(stations))
     vmem = pl.BlockSpec(memory_space=pltpu.VMEM)
@@ -208,13 +199,13 @@
             jax.ShapeDtypeStruct(weights.shape, jnp.bfloat16),
             jax.ShapeDtypeStruct(spread.shape, jnp.bfloat16),
         ],
-        in_specs=[hbm, hbm, pl.BlockSpec(memory_space=pltpu.SMEM)] + [hbm] * 6,
+        in_specs=[hbm, hbm, pl.BlockSpec(memory_space=pltpu.SMEM)] + [hbm] * 4,
         out_specs=[vmem] * 3,
         scratch_shapes=held
         + [
             pltpu.VMEM((2 * LANES, CHANNELS), jnp.bfloat16),
             pltpu.VMEM((2, FIRST * POLS * SPECTRA, LANES), jnp.float32),
-            pltpu.SemaphoreType.DMA((9,)),
+            pltpu.SemaphoreType.DMA((6,)),
         ],
         compiler_params=pltpu.CompilerParams(vmem_limit_bytes=20 * 2**20),
         name="channelize",

time: 48.3 us -> 48.2 us (level)
  no operation moved by 1% of the time
where the time goes in v5:
time: 48.2 us; the launch traced here: 48 us
  blocking collectives  42.3 us (88%)
  Pallas kernels  4.98 us (10%)
  between operations  0.67 us (1%)
    all_to_all x2, blocking collectives, exchange(): lax.all_to_all(blocks, axis, split_axis=0, concat_axis=0, axis_index_grou...  42.3 us
    pallas_call x1, Pallas kernels, channelize(): pl.pallas_call(channel_kernel, out_shape=[jax.ShapeDtypeStruct((CHANNELS...  2.66 us
    pallas_call x1, Pallas kernels, beamform(): pl.pallas_call(beam_kernel, out_shape=jax.ShapeDtypeStruct((BEAMS // 8, 8...  1.42 us

profile of v5, /device:TPU:60, one launch (start us, length us, event | category | flops | bytes accessed | tf_op | source)
XLA Modules:
  0.0 48.0 jit_solution(5116168167919282308)
XLA Ops:
  0.7 2.7 %channelize.1 = (bf16[32,16,128]{2,1,0:T(8,128)(2,1)S(1)}, bf16[32,256,128]{2,1,0:T(8,128)(2,1)S(1)}, bf16[128,2048]{1,0:T(8,128)(2,1)S(1)}) custom-call(bf16[2,1216,128]{2,1,0:T(8,128)(2,1)} %bitcast.8, s32[32,128]{1,0:T(8,128)} %bitcast.9, s32[1]{0:T(128)S(6)} %copy.9.live_ref, f32[17,64,128]{2,1,0:T(8,128)} %constant.6.clone.taps_hbm, ...), custom_call_target="tpu_custom_call" | custom-call | tf_op jit(solution)/shard_map/channelize/pallas_call | solution.py:195
  3.3 23.6 %all_to_all.10.x_ref = bf16[32,16,128]{2,1,0:T(8,128)(2,1)S(1)} all-to-all(bf16[32,16,128]{2,1,0:T(8,128)(2,1)S(1)} %get-tuple-element.8), channel_id=1, replica_groups={{30,0,1,2,3,4,5,6,7,8,9,10,11,12,13,14,15,16,17,18,19,20,21,22,23,24,25..., dimensions={0} | all-to-all | bytes 262144 | tf_op jit(solution)/shard_map/all_to_all | solution.py:326
  26.9 1.4 %beamform.1 = bf16[16,128,128]{2,1,0:T(8,128)(2,1)S(1)} custom-call(bf16[32,16,128]{2,1,0:T(8,128)(2,1)S(1)} %all_to_all.10.x_ref, bf16[32,256,128]{2,1,0:T(8,128)(2,1)S(1)} %get-tuple-element.9.w_ref, bf16[128,2048]{1,0:T(8,128)(2,1)S(1)} %get-tuple-element.10.spread_ref), custom_call_target="tpu_custom_call" | custom-call | tf_op jit(solution)/shard_map/beamform/pallas_call | solution.py:271
  28.3 18.8 %all_to_all.11.x_ref = bf16[16,128,128]{2,1,0:T(8,128)(2,1)S(1)} all-to-all(bf16[16,128,128]{2,1,0:T(8,128)(2,1)S(1)} %beamform.1), channel_id=1, replica_groups={{320,0,32,64,96,128,160,192,224,256,288,352,384,416,448,480},{321,1,33,..., dimensions={0} | all-to-all | bytes 1048576 | tf_op jit(solution)/shard_map/all_to_all | solution.py:326
  47.1 0.9 %sum_groups.1 = f32[8,2,2,4,128]{4,3,2,1,0:T(4,128)} custom-call(bf16[16,128,128]{2,1,0:T(8,128)(2,1)S(1)} %all_to_all.11.x_ref), custom_call_target="tpu_custom_call" | custom-call | tf_op jit(solution)/shard_map/sum_groups/pallas_call | solution.py:314

commit v6 on v5

--- a/solution.py
+++ b/solution.py
@@ -63,14 +63,12 @@
 
 
 def spread_matrix(stations):
-    out = np.zeros((POLS, 2, stations, 2, POLS, stations, WIDE, 2), np.float32)
+    out = np.zeros((POLS, 2, stations, POLS, stations, WIDE, 2), np.float32)
     for p in range(POLS):
         for i, st in enumerate(leading(CHAN_LEAD, stations)):
-            out[p, 0, i, 0, p, st, :, 0] = 1.0
-            out[p, 1, i, 0, p, st, :, 1] = -1.0
-            out[p, 1, i, 1, p, st, :, 0] = 1.0
-            out[p, 0, i, 1, p, st, :, 1] = 1.0
-    return out.reshape(POLS * 2 * stations, 4 * stations * WIDE * 2).astype(jnp.bfloat16)
+            out[p, 0, i, p, st, :, 0] = 1.0
+            out[p, 1, i, p, st, :, 1] = -1.0
+    return out.reshape(POLS * 2 * stations, POLS * stations * WIDE * 2).astype(jnp.bfloat16)
 
 
 def channel_kernel(
@@ -226,41 +224,56 @@
                 rows.append(wide_ref[pl.ds(start, stations, stride=PARTS), :])
         turned.append(jnp.concatenate(rows, 0).T)
     depth = stations * WIDE * 2
-    row_slot = lax.broadcasted_iota(jnp.int32, (SPECTRA * WIDE, depth), 0) % WIDE
-    column_slot = lax.broadcasted_iota(jnp.int32, (SPECTRA * WIDE, depth), 1) // 2 % WIDE
+    height = SPECTRA * WIDE
+    row_slot = lax.broadcasted_iota(jnp.int32, (height, depth), 0) % WIDE
+    column_slot = lax.broadcasted_iota(jnp.int32, (height, depth), 1) // 2 % WIDE
     meets = row_slot == column_slot
-    together = 16
-    height = SPECTRA * WIDE
-    for batch in range(groups // together):
-        small = []
-        for g in range(batch * together, (batch + 1) * together):
+    by_product = POLS
+    small = []
+    for g in range(groups):
+        for s in range(SPECTRA):
+            small.append(turned[s][g * WIDE : (g + 1) * WIDE])
+    spread = jnp.dot(
+        jnp.concatenate(small, 0).astype(bf16),
+        spread_ref[...],
+        preferred_element_type=f32,
+    )
+    lane = lax.broadcasted_iota(jnp.int32, (LANES, LANES), 1)
+    held = LANES // (2 * WIDE)
+    moved = {}
+    for b in range(by_product, 2 * POLS):
+        p = b % POLS
+        for c in range(depth // LANES):
+            station = c * held + lane // (2 * WIDE)
+            at = jnp.where(station < CHAN_LEAD, station + 1, station)
+            at = jnp.where(station == CHAN_LEAD, 0, at)
+            index = (p * 2 + 1 - lane % 2) * stations + at
             for s in range(SPECTRA):
-                small.append(turned[s][g * WIDE : (g + 1) * WIDE])
-        spread = jnp.dot(
-            jnp.concatenate(small, 0).astype(bf16), spread_ref[...], preferred_element_type=f32
-        )
-        beams = []
-        for i in range(together):
-            g = batch * together + i
-            lhs = jnp.concatenate(
-                [
-                    jnp.where(
-                        meets,
-                        spread[i * height : (i + 1) * height, b * depth : (b + 1) * depth],
-                        0.0,
-                    ).astype(bf16)
-                    for b in range(2 * POLS)
-                ],
-                0,
-            )
-            weights = w_ref[:, g * 2 * WIDE : (g + 1) * 2 * WIDE, :].reshape(depth, BEAMS)
-            product = jnp.dot(lhs, weights, preferred_element_type=f32)
-            beams.append(product.T)
-        for pair in range(together // 2):
-            where = (batch * together // 2 + pair) * 16
+                moved[b, c, s] = jnp.take_along_axis(turned[s], index, axis=1)
+    beams = []
+    for g in range(groups):
+        here = slice(g * WIDE, (g + 1) * WIDE)
+        blocks = []
+        for b in range(2 * POLS):
+            if b < by_product:
+                block = spread[g * height : (g + 1) * height, b * depth : (b + 1) * depth]
+            else:
+                block = jnp.concatenate(
+                    [
+                        jnp.concatenate([moved[b, c, s][here] for s in range(SPECTRA)], 0)
+                        for c in range(depth // LANES)
+                    ],
+                    1,
+                )
+            blocks.append(jnp.where(meets, block, 0.0).astype(bf16))
+        weights = w_ref[:, g * 2 * WIDE : (g + 1) * 2 * WIDE, :].reshape(depth, BEAMS)
+        product = jnp.dot(jnp.concatenate(blocks, 0), weights, preferred_element_type=f32)
+        beams.append(product.T)
+        if g % 2:
+            where = g // 2 * 16
             for i, b in enumerate(leading(GRP_LEAD, out_ref.shape[0])):
                 out_ref[i, where : where + 16, :] = jnp.concatenate(
-                    [beams[2 * pair + d][8 * b : 8 * b + 8] for d in range(2)], 0
+                    [beams[g - 1 + d][8 * b : 8 * b + 8] for d in range(2)], 0
                 ).astype(bf16)
 
 

time: 48.2 us -> 48 us (level)
  no operation moved by 1% of the time
where the time goes in v6:
time: 48 us; the launch traced here: 47.7 us
  blocking collectives  42.3 us (88%)
  Pallas kernels  4.73 us (10%)
  between operations  0.67 us (1%)
    all_to_all x2, blocking collectives, exchange(): lax.all_to_all(blocks, axis, split_axis=0, concat_axis=0, axis_index_grou...  42.3 us
    pallas_call x1, Pallas kernels, channelize(): pl.pallas_call(channel_kernel, out_shape=[jax.ShapeDtypeStruct((CHANNELS...  2.66 us
    pallas_call x1, Pallas kernels, beamform(): pl.pallas_call(beam_kernel, out_shape=jax.ShapeDtypeStruct((BEAMS // 8, 8...  1.17 us

profile of v6, /device:TPU:60, one launch (start us, length us, event | category | flops | bytes accessed | tf_op | source)
XLA Modules:
  0.0 47.7 jit_solution(463747267569483205)
XLA Ops:
  0.7 2.7 %channelize.1 = (bf16[32,16,128]{2,1,0:T(8,128)(2,1)S(1)}, bf16[32,256,128]{2,1,0:T(8,128)(2,1)S(1)}, bf16[128,1024]{1,0:T(8,128)(2,1)S(1)}) custom-call(bf16[2,1216,128]{2,1,0:T(8,128)(2,1)} %bitcast.8, s32[32,128]{1,0:T(8,128)} %bitcast.9, s32[1]{0:T(128)S(6)} %copy.9.live_ref, f32[17,64,128]{2,1,0:T(8,128)} %constant.6.clone.taps_hbm, ...), custom_call_target="tpu_custom_call" | custom-call | tf_op jit(solution)/shard_map/channelize/pallas_call | solution.py:193
  3.3 23.6 %all_to_all.10.x_ref = bf16[32,16,128]{2,1,0:T(8,128)(2,1)S(1)} all-to-all(bf16[32,16,128]{2,1,0:T(8,128)(2,1)S(1)} %get-tuple-element.8), channel_id=1, replica_groups={{30,0,1,2,3,4,5,6,7,8,9,10,11,12,13,14,15,16,17,18,19,20,21,22,23,24,25..., dimensions={0} | all-to-all | bytes 262144 | tf_op jit(solution)/shard_map/all_to_all | solution.py:339
  26.9 1.2 %beamform.1 = bf16[16,128,128]{2,1,0:T(8,128)(2,1)S(1)} custom-call(bf16[32,16,128]{2,1,0:T(8,128)(2,1)S(1)} %all_to_all.10.x_ref, bf16[32,256,128]{2,1,0:T(8,128)(2,1)S(1)} %get-tuple-element.9.w_ref, bf16[128,1024]{1,0:T(8,128)(2,1)S(1)} %get-tuple-element.10.spread_ref), custom_call_target="tpu_custom_call" | custom-call | tf_op jit(solution)/shard_map/beamform/pallas_call | solution.py:284
  28.0 18.8 %all_to_all.11.x_ref = bf16[16,128,128]{2,1,0:T(8,128)(2,1)S(1)} all-to-all(bf16[16,128,128]{2,1,0:T(8,128)(2,1)S(1)} %beamform.1), channel_id=1, replica_groups={{320,0,32,64,96,128,160,192,224,256,288,352,384,416,448,480},{321,1,33,..., dimensions={0} | all-to-all | bytes 1048576 | tf_op jit(solution)/shard_map/all_to_all | solution.py:339
  46.8 0.9 %sum_groups.1 = f32[8,2,2,4,128]{4,3,2,1,0:T(4,128)} custom-call(bf16[16,128,128]{2,1,0:T(8,128)(2,1)S(1)} %all_to_all.11.x_ref), custom_call_target="tpu_custom_call" | custom-call | tf_op jit(solution)/shard_map/sum_groups/pallas_call | solution.py:327

commit v7 on v6

--- a/solution.py
+++ b/solution.py
@@ -87,7 +87,6 @@
     taps_ref,
     matrix_ref,
     pick_ref,
-    folded_ref,
     sem,
 ):
     f32, bf16 = jnp.float32, jnp.bfloat16
@@ -135,12 +134,15 @@
         matrix_ref[:ROWS], jnp.concatenate([columns, columns], 0), preferred_element_type=f32
     )
     cosine, sine = taps_ref[TAPS, :FIRST], taps_ref[TAPS, FIRST:]
+    halves = [[], []]
     for i in range(count):
         real = first[:FIRST, i * LANES : (i + 1) * LANES]
         imag = first[FIRST:, i * LANES : (i + 1) * LANES]
-        folded_ref[0, pl.ds(i, FIRST, stride=count), :] = real * cosine + imag * sine
-        folded_ref[1, pl.ds(i, FIRST, stride=count), :] = imag * cosine - real * sine
-    folded = jnp.concatenate([folded_ref[0], folded_ref[1]], 1).astype(bf16)
+        halves[0].append(real * cosine + imag * sine)
+        halves[1].append(imag * cosine - real * sine)
+    folded = jnp.concatenate(
+        [jnp.swapaxes(jnp.stack(h, 0), 0, 1).reshape(FIRST * count, LANES) for h in halves], 1
+    ).astype(bf16)
     second = jnp.concatenate([matrix_ref[ROWS : 5 * LANES // 2], matrix_ref[5 * LANES // 2 :]], 1)
     spectrum = jnp.dot(folded, second, preferred_element_type=f32)
     spectrum = spectrum.astype(bf16).astype(f32) * live_ref[0].astype(f32)
@@ -202,7 +204,6 @@
         scratch_shapes=held
         + [
             pltpu.VMEM((2 * LANES, CHANNELS), jnp.bfloat16),
-            pltpu.VMEM((2, FIRST * POLS * SPECTRA, LANES), jnp.float32),
             pltpu.SemaphoreType.DMA((6,)),
         ],
         compiler_params=pltpu.CompilerParams(vmem_limit_bytes=20 * 2**20),
@@ -268,7 +269,7 @@
             blocks.append(jnp.where(meets, block, 0.0).astype(bf16))
         weights = w_ref[:, g * 2 * WIDE : (g + 1) * 2 * WIDE, :].reshape(depth, BEAMS)
         product = jnp.dot(jnp.concatenate(blocks, 0), weights, preferred_element_type=f32)
-        beams.append(product.T)
+        beams.append(product.astype(bf16).T.astype(f32))
         if g % 2:
             where = g // 2 * 16
             for i, b in enumerate(leading(GRP_LEAD, out_ref.shape[0])):

time: 48 us -> 47.9 us (level)
  no operation moved by 1% of the time
where the time goes in v7:
time: 47.9 us; the launch traced here: 47.7 us
  blocking collectives  42.3 us (88%)
  Pallas kernels  4.71 us (10%)
  between operations  0.67 us (1%)
    all_to_all x2, blocking collectives, exchange(): lax.all_to_all(blocks, axis, split_axis=0, concat_axis=0, axis_index_grou...  42.3 us
    pallas_call x1, Pallas kernels, channelize(): pl.pallas_call(channel_kernel, out_shape=[jax.ShapeDtypeStruct((CHANNELS...  2.67 us
    pallas_call x1, Pallas kernels, beamform(): pl.pallas_call(beam_kernel, out_shape=jax.ShapeDtypeStruct((BEAMS // 8, 8...  1.13 us

profile of v7, /device:TPU:60, one launch (start us, length us, event | category | flops | bytes accessed | tf_op | source)
XLA Modules:
  0.0 47.7 jit_solution(880074480459840984)
XLA Ops:
  0.7 2.7 %channelize.1 = (bf16[32,16,128]{2,1,0:T(8,128)(2,1)S(1)}, bf16[32,256,128]{2,1,0:T(8,128)(2,1)S(1)}, bf16[128,1024]{1,0:T(8,128)(2,1)S(1)}) custom-call(bf16[2,1216,128]{2,1,0:T(8,128)(2,1)} %bitcast.8, s32[32,128]{1,0:T(8,128)} %bitcast.9, s32[1]{0:T(128)S(6)} %copy.9.live_ref, f32[17,64,128]{2,1,0:T(8,128)} %constant.6.clone.taps_hbm, ...), custom_call_target="tpu_custom_call" | custom-call | tf_op jit(solution)/shard_map/channelize/pallas_call | solution.py:195
  3.3 23.6 %all_to_all.10.x_ref = bf16[32,16,128]{2,1,0:T(8,128)(2,1)S(1)} all-to-all(bf16[32,16,128]{2,1,0:T(8,128)(2,1)S(1)} %get-tuple-element.8), channel_id=1, replica_groups={{30,0,1,2,3,4,5,6,7,8,9,10,11,12,13,14,15,16,17,18,19,20,21,22,23,24,25..., dimensions={0} | all-to-all | bytes 262144 | tf_op jit(solution)/shard_map/all_to_all | solution.py:340
  26.9 1.1 %beamform.1 = bf16[16,128,128]{2,1,0:T(8,128)(2,1)S(1)} custom-call(bf16[32,16,128]{2,1,0:T(8,128)(2,1)S(1)} %all_to_all.10.x_ref, bf16[32,256,128]{2,1,0:T(8,128)(2,1)S(1)} %get-tuple-element.9.w_ref, bf16[128,1024]{1,0:T(8,128)(2,1)S(1)} %get-tuple-element.10.spread_ref), custom_call_target="tpu_custom_call" | custom-call | tf_op jit(solution)/shard_map/beamform/pallas_call | solution.py:285
  28.0 18.8 %all_to_all.11.x_ref = bf16[16,128,128]{2,1,0:T(8,128)(2,1)S(1)} all-to-all(bf16[16,128,128]{2,1,0:T(8,128)(2,1)S(1)} %beamform.1), channel_id=1, replica_groups={{320,0,32,64,96,128,160,192,224,256,288,352,384,416,448,480},{321,1,33,..., dimensions={0} | all-to-all | bytes 1048576 | tf_op jit(solution)/shard_map/all_to_all | solution.py:340
  46.8 0.9 %sum_groups.1 = f32[8,2,2,4,128]{4,3,2,1,0:T(4,128)} custom-call(bf16[16,128,128]{2,1,0:T(8,128)(2,1)S(1)} %all_to_all.11.x_ref), custom_call_target="tpu_custom_call" | custom-call | tf_op jit(solution)/shard_map/sum_groups/pallas_call | solution.py:328

commit v8 on v7

--- a/solution.py
+++ b/solution.py
@@ -20,7 +20,7 @@
 PARTS = 2 * POLS * SPECTRA
 HALF = FIRST // 2
 WIDE = 8
-CHAN_LEAD = 30
+CHAN_LEAD = 31
 GRP_LEAD = 10
 
 

time: 47.9 us -> 47.9 us (level)
  no operation moved by 1% of the time
where the time goes in v8:
time: 47.9 us; the launch traced here: 47.6 us
  blocking collectives  42.3 us (88%)
  Pallas kernels  4.71 us (10%)
  between operations  0.67 us (1%)
    all_to_all x2, blocking collectives, exchange(): lax.all_to_all(blocks, axis, split_axis=0, concat_axis=0, axis_index_grou...  42.3 us
    pallas_call x1, Pallas kernels, channelize(): pl.pallas_call(channel_kernel, out_shape=[jax.ShapeDtypeStruct((CHANNELS...  2.67 us
    pallas_call x1, Pallas kernels, beamform(): pl.pallas_call(beam_kernel, out_shape=jax.ShapeDtypeStruct((BEAMS // 8, 8...  1.14 us

profile of v8, /device:TPU:60, one launch (start us, length us, event | category | flops | bytes accessed | tf_op | source)
XLA Modules:
  0.0 47.6 jit_solution(9478911367753687155)
XLA Ops:
  0.7 2.7 %channelize.1 = (bf16[32,16,128]{2,1,0:T(8,128)(2,1)S(1)}, bf16[32,256,128]{2,1,0:T(8,128)(2,1)S(1)}, bf16[128,1024]{1,0:T(8,128)(2,1)S(1)}) custom-call(bf16[2,1216,128]{2,1,0:T(8,128)(2,1)} %bitcast.8, s32[32,128]{1,0:T(8,128)} %bitcast.9, s32[1]{0:T(128)S(6)} %copy.9.live_ref, f32[17,64,128]{2,1,0:T(8,128)} %constant.6.clone.taps_hbm, ...), custom_call_target="tpu_custom_call" | custom-call | tf_op jit(solution)/shard_map/channelize/pallas_call | solution.py:195
  3.3 23.3 %all_to_all.10.x_ref = bf16[32,16,128]{2,1,0:T(8,128)(2,1)S(1)} all-to-all(bf16[32,16,128]{2,1,0:T(8,128)(2,1)S(1)} %get-tuple-element.8), channel_id=1, replica_groups={{31,0,1,2,3,4,5,6,7,8,9,10,11,12,13,14,15,16,17,18,19,20,21,22,23,24,25..., dimensions={0} | all-to-all | bytes 262144 | tf_op jit(solution)/shard_map/all_to_all | solution.py:340
  26.6 1.1 %beamform.1 = bf16[16,128,128]{2,1,0:T(8,128)(2,1)S(1)} custom-call(bf16[32,16,128]{2,1,0:T(8,128)(2,1)S(1)} %all_to_all.10.x_ref, bf16[32,256,128]{2,1,0:T(8,128)(2,1)S(1)} %get-tuple-element.9.w_ref, bf16[128,1024]{1,0:T(8,128)(2,1)S(1)} %get-tuple-element.10.spread_ref), custom_call_target="tpu_custom_call" | custom-call | tf_op jit(solution)/shard_map/beamform/pallas_call | solution.py:285
  27.7 19.0 %all_to_all.11.x_ref = bf16[16,128,128]{2,1,0:T(8,128)(2,1)S(1)} all-to-all(bf16[16,128,128]{2,1,0:T(8,128)(2,1)S(1)} %beamform.1), channel_id=1, replica_groups={{320,0,32,64,96,128,160,192,224,256,288,352,384,416,448,480},{321,1,33,..., dimensions={0} | all-to-all | bytes 1048576 | tf_op jit(solution)/shard_map/all_to_all | solution.py:340
  46.7 0.9 %sum_groups.1 = f32[8,2,2,4,128]{4,3,2,1,0:T(4,128)} custom-call(bf16[16,128,128]{2,1,0:T(8,128)(2,1)S(1)} %all_to_all.11.x_ref), custom_call_target="tpu_custom_call" | custom-call | tf_op jit(solution)/shard_map/sum_groups/pallas_call | solution.py:328
